TPU v7x, 32 devices: a whole 2x2x4 slice. The times are simulated.
32 devices in a mesh: groups: 2 (over y), pool: 16 (over z, x, core).
Axes of the slice: x: 2, y: 2, z: 4, core: 2. Of those that a mesh axis runs over, the one named last changes fastest.
Arguments:
- anchors: bfloat16 [4096, 1024], P(('groups', 'pool')), parts along dimension 0, may hold values from -7 to 7
- deltas: bfloat16 [4096, 15, 1024], P(('groups', 'pool')), parts along dimension 0, may hold values from -5 to 5
- scales: float32 [4096, 8], P(('groups', 'pool')), parts along dimension 0, may hold values from 0.15 to 0.8
- queries: bfloat16 [32, 8, 8192], P('groups'), parts along dimension 0, may hold values from -7 to 7
- lengths: int32 [32], P('groups'), parts along dimension 0, may hold values from 64 to 192, as said below
- page_owner: int32 [4096], P('groups'), parts along dimension 0, may hold values from 0 to 15, as said below
Outputs:
- decoded_cache: bfloat16 [4096, 16, 1024], P(('groups', 'pool')), parts along dimension 0
- attention: bfloat16 [32, 8, 8192], P('groups', None, 'pool'), parts along dimension 0
There are 2 independent parts, one for each index of `groups`. A program takes and returns all parts, laid end to end along the dimension named above; each array names one. Nothing has to cross between parts.
Inputs may be any that keep to these rules, and one draw needn't show every extreme that they name: `lengths`: pages of each request; together they cover all 2048 pages of the group. `page_owner`: each prefill device sends either none or exactly 16 of its pages to each decode device, and each decode device owns exactly 128 pages.
All inputs are finite; a program needn't handle non-finite values.
Results may differ from a plain program's by a relative error of at most 0.0046.
Values may be sent and summed in bfloat16 or wider, within the bound.
No kernel may reach another device: no remote copies, remote signals or barrier semaphores. Data moves between devices by JAX's collectives and lax.ppermute only.
A program may use at most 192 MiB of HBM per device.

v0:
```python
import jax
import jax.numpy as jnp
from jax import lax
from jax.sharding import PartitionSpec as P

QH = 64
KVH = 4
HD = 128
PAGE = 16
STEPS = 8
REQS = 16


def decode_pages(anchors, deltas, scales):
    block_scale = jnp.repeat(scales, HD, axis=1)
    rebuilt = anchors[:, None, :].astype(jnp.float32) + block_scale[:, None, :] * deltas.astype(
        jnp.float32
    )
    return jnp.concatenate([anchors[:, None, :], rebuilt.astype(jnp.bfloat16)], axis=1)


def page_scores(work_pages, queries, requests):
    number = work_pages.shape[0]
    key_rows = work_pages[:, :, : KVH * HD].reshape(number, PAGE, KVH, HD)
    picked = jnp.take(queries, requests, axis=0).reshape(number, STEPS, KVH, QH // KVH, HD)
    scores = jnp.einsum(
        "nskgd,ntkd->nskgt", picked, key_rows, preferred_element_type=jnp.float32
    ) * HD ** (-0.5)
    return (scores, jnp.max(scores, axis=4))


def accumulate(scores, page_max, work_pages, requests, shift_max):
    number = work_pages.shape[0]
    rows_out = shift_max.shape[0]
    block_size = min(32, number)
    blocks = number // block_size
    value_rows = work_pages[:, :, KVH * HD :].reshape(blocks, block_size, PAGE, KVH, HD)
    score_blocks = scores.reshape((blocks, block_size) + scores.shape[1:])
    max_blocks = page_max.reshape((blocks, block_size) + page_max.shape[1:])
    request_blocks = requests.reshape(blocks, block_size)

    def block_step(running, pieces):
        totals, numerator = running
        block_scores, block_max, block_values, block_requests = pieces
        exponent = jnp.exp(block_scores - block_max[..., None])
        weights = exponent.astype(jnp.bfloat16)
        page_out = jnp.einsum(
            "nskgt,ntkd->nskgd", weights, block_values, preferred_element_type=jnp.float32
        )
        factor = jnp.exp(block_max - jnp.take(shift_max, block_requests, axis=0))
        select = (block_requests[None, :] == jnp.arange(rows_out, dtype=jnp.int32)[:, None]).astype(
            jnp.float32
        )
        spread = select[:, :, None, None, None] * factor[None]
        totals = totals + jnp.sum(spread * jnp.sum(exponent, axis=4)[None], axis=1)
        numerator = numerator + jnp.einsum(
            "rnskg,nskgd->rskgd", spread, page_out, precision=lax.Precision.HIGHEST
        )
        return ((totals, numerator), None)

    start_totals = jnp.zeros(shift_max.shape, jnp.float32)
    start_numer = jnp.zeros(shift_max.shape + (HD,), jnp.float32)
    finals, ignored = lax.scan(
        block_step,
        (start_totals, start_numer),
        (score_blocks, max_blocks, value_rows, request_blocks),
    )
    return finals


def request_of(index, request_ends):
    return jnp.sum((index[:, None] >= request_ends[None, :]).astype(jnp.int32), axis=1)


def local(anchors, deltas, scales, queries, lengths, page_owner):
    devices = lax.axis_size("pool")
    position = lax.axis_index("pool")
    number = anchors.shape[0]
    capacity = max(2, 2 * number // devices)
    pages = decode_pages(anchors, deltas, scales)
    request_ends = jnp.cumsum(lengths)
    owners = lax.dynamic_slice_in_dim(page_owner, position * number, number, 0)
    marked = (owners[:, None] == jnp.arange(devices, dtype=jnp.int32)[None, :]).astype(jnp.int32)
    ranking = jnp.sum((jnp.cumsum(marked, axis=0) - 1) * marked, axis=1)
    slot_ids = owners * capacity + ranking
    matches = slot_ids[None, :] == jnp.arange(devices * capacity, dtype=jnp.int32)[:, None]
    sources = jnp.sum(jnp.where(matches, jnp.arange(number, dtype=jnp.int32)[None, :], 0), axis=1)
    outgoing = jnp.take(pages, sources, axis=0)
    arrived = lax.all_to_all(outgoing, "pool", split_axis=0, concat_axis=0, tiled=True)
    held_pages = jnp.nonzero(page_owner == position, size=number)[0].astype(jnp.int32)
    senders = held_pages // number
    before = jnp.sum((held_pages[None, :] < (senders * number)[:, None]).astype(jnp.int32), axis=1)
    row_ids = senders * capacity + jnp.arange(number, dtype=jnp.int32) - before
    cache = jnp.take(arrived, row_ids, axis=0)
    columns = QH * HD // devices
    requests = request_of(held_pages, request_ends)
    scores, page_max = page_scores(cache, queries, requests)
    onehot = requests[None, :] == jnp.arange(REQS, dtype=jnp.int32)[:, None]
    local_max = jnp.max(jnp.where(onehot[:, :, None, None, None], page_max[None], -1e30), axis=1)
    global_max = lax.pmax(local_max.astype(jnp.bfloat16), "pool").astype(local_max.dtype)
    totals, numerator = accumulate(scores, page_max, cache, requests, global_max)
    summed, numerator = lax.psum((totals, numerator), "pool")
    whole = (numerator / summed[..., None]).reshape(REQS, STEPS, QH * HD)
    result = lax.dynamic_slice_in_dim(whole, position * columns, columns, 2)
    return (cache, result.astype(jnp.bfloat16))


def solution(mesh):
    placed = (
        P(("groups", "pool"), None),
        P(("groups", "pool"), None, None),
        P(("groups", "pool"), None),
        P("groups", None, None),
        P("groups"),
        P("groups"),
    )
    return jax.shard_map(
        local,
        mesh=mesh,
        in_specs=placed,
        out_specs=(P(("groups", "pool"), None, None), P("groups", None, "pool")),
        check_vma=False,
    )
```

profile of v0, /device:TPU:11, one launch (start us, length us, event | category | flops | bytes accessed | tf_op | source)
XLA Modules:
  0.0 683.2 jit_solution(6491035517801411600)
XLA Ops:
  7.2 0.9 copy.88
  8.4 1.8 convert_element_type.46
  10.2 1.4 copy.90
  12.8 0.8 multiply_add_fusion
  13.7 5.1 add_convert_fusion
  18.8 3.4 pad_maximum_fusion
  22.2 10.8 %gather_fusion.1 = bf16[256,16,1024]{2,1,0:T(8,128)(2,1)} fusion(bf16[128,16,1024]{2,1,0:T(8,128)(2,1)} %pad_maximum_fusion, s32[1024]{0:T(1024)S(1)} %pad_clamp_fusion.3), kind=kCustom, calls=%fused_computation.1 | custom fusion | bytes 16778240 | tf_op jit(solution)/shard_map/jit(_take)/gather | solution.py:88
  33.0 7.5 %broadcast_select_fusion = bf16[256,16,1024]{2,1,0:T(8,128)(2,1)} fusion(bf16[256,16,1024]{2,1,0:T(8,128)(2,1)} %gather_fusion.1, pred[256]{0:T(512)(128)(4,1)S(1)} %compare_and_fusion.2), kind=kLoop, calls=%fused_computation.45 | loop fusion | flops 4194304 | bytes 16777472 | tf_op jit(solution)/shard_map/jit(_take)/select_n | solution.py:88
  40.5 6.7 all-to-all-start
  48.5 14.9 %scatter_custom_fusion = s32[128]{0:T(128)S(1)} fusion(s32[2048]{0:T(1024)S(1)} %bitcast.93, s32[2048]{0:T(1024)S(1)} %broadcast.455, s32[]{:T(128)} %constant.141.clone.1), kind=kCustom, calls=%fused_computation.107 | custom fusion | flops 2048 | bytes 516 | tf_op jit(solution)/shard_map/scatter-add | solution.py:90
  65.5 8.4 %gather_fusion.3 = bf16[128,8,8192]{2,1,0:T(8,128)(2,1)} fusion(bf16[16,8,8192]{2,1,0:T(8,128)(2,1)S(1)} %copy-done, s32[1024]{0:T(1024)S(1)} %pad_clamp_fusion.1), kind=kCustom, calls=%fused_computation.3 | custom fusion | bytes 33554944 | tf_op jit(solution)/shard_map/jit(_take)/gather | solution.py:25
  73.9 0.8 fusion.36
  74.8 154.8 %all-to-all-done = bf16[256,16,1024]{2,1,0:T(8,128)(2,1)} async-done(((bf16[256,16,1024]{2,1,0:T(8,128)(2,1)}), bf16[256,16,1024]{2,1,0:T(8,128)(2,1)}, u32[]{:S(2)}, u32[]{:S(2)}) %all-to-all-start) | async-done | bytes 8388640 | tf_op jit(solution)/shard_map/all_to_all | solution.py:89
  229.6 6.2 gather_fusion.2
  235.8 2.6 broadcast_select_fusion.1
  238.4 2.8 fusion.43
  241.7 3.5 copy.93
  245.1 3.0 copy.107
  248.2 58.1 %bitcast_reduce_fusion = (f32[128,8,4,16]{3,1,2,0:T(8,128)S(1)}, f32[128,4,16,8,16]{4,2,3,1,0:T(8,128)}) fusion(bf16[128,16,4,128,1]{3,1,4,2,0:T(8,128)(2,1)} %copy.107, bf16[128,8,4,16,128]{4,1,3,2,0:T(8,128)(2,1)} %bitcast.85, pred[128]{0:T(512)(128)(4,1)S(1)} %compare_and_fusion.1), kind=kOutput, calls=%fused_computation.38 | convolution fusion | flops 278855680 | bytes 23330944 | tf_op jit(solution)/shard_map/nskgd,ntkd->nskgt/dot_general | solution.py:26
  306.3 1.0 copy.100
  307.3 1.4 select_reduce_fusion
  308.7 44.2 %pmax.7 = bf16[16,8,4,16]{3,2,1,0:T(4,128)(2,1)S(1)} all-reduce(bf16[16,8,4,16]{3,2,1,0:T(4,128)(2,1)S(1)} %select_reduce_fusion), channel_id=1, replica_groups=mesh['groups'=2,'pool'=16] {'pool'}, use_global_device_ids=true, to_apply=%region_13.14 | all-reduce | flops 8192 | bytes 32768 | tf_op jit(solution)/shard_map/pmax | solution.py:100
  352.9 4.0 reshape.392
  356.9 188.3 %while.13 = (s32[]{:T(128)}, f32[16,8,4,16]{0,3,2,1:T(8,128)S(1)}, f32[16,8,4,16,128]{4,0,3,2,1:T(8,128)}, s32[4,32]{1,0:T(4,128)S(1)}, f32[4,32,8,4,16]{4,2,3,1...) while((s32[]{:T(128)}, f32[16,8,4,16]{0,3,2,1:T(8,128)S(1)}, ...), condition=%wide.region_17.18_spmd.clone, body=%wide.region_14.17_spmd.clone.sunk | while | flops 473983264 | bytes 67775624 | solution.py:63
  356.9 7.7 %constant_dynamic-slice_fusion.5 = f32[1,32,8,4,16,16]{4,5,2,3,1,0:T(8,128)} fusion(f32[4,32,8,4,16,16]{4,5,2,3,1,0:T(8,128)} %get-tuple-element.226, s32[]{:T(128)S(6)} %copy.143), kind=kLoop, calls=%fused_computation.34.clone.1 | loop fusion | bytes 2097156 | tf_op jit(solution)/shard_map/while/body/jit(dynamic_index_in_dim)/dynamic_slice | solution.py:63
  364.6 9.0 %copy.137 = f32[1,32,8,4,16,16]{5,4,2,3,1,0:T(8,128)} copy(f32[1,32,8,4,16,16]{4,5,2,3,1,0:T(8,128)} %constant_dynamic-slice_fusion.5) | data formatting | bytes 2097152 | tf_op jit(solution)/shard_map/while/body/jit(dynamic_index_in_dim)/dynamic_slice | solution.py:63
  374.3 1.2 fusion.58
  375.5 6.9 %fusion.59 = f32[32,8,4,16]{3,1,2,0:T(8,128)S(1)} fusion(f32[1,32,8,4,16,16]{5,4,2,3,1,0:T(8,128)} %copy.137, f32[32,8,4,16]{3,1,2,0:T(8,128)S(1)} %get-tuple-element.197), kind=kLoop, calls=%fused_computation.10.clone.1 | loop fusion | flops 507904 | bytes 1179648 | tf_op jit(solution)/shard_map/while/body/eval_jaxpr/reduce_sum | solution.py:55
  383.0 1.2 fusion.61
  384.3 1.3 constant_dynamic-slice_fusion.6
  385.6 5.7 fusion.62
  391.3 10.8 %bitcast_add_fusion.2 = f32[16,8,4,16,128]{4,0,3,2,1:T(8,128)S(1)} fusion(f32[16,8,4,16,128]{4,0,3,2,1:T(8,128)S(1)} %copy-done.2, f32[32,8,4,16,128]{4,3,1,2,0:T(8,128)S(1)} %fusion.62, f32[32,8,4,16]{0,3,2,1:T(8,128)S(1)} %copy.139, f32[16,32]{1,0:T(8,128)S(1)} %fusion.60, pred[]{:T(512)S(6)} %compare.44), kind=kOutput, calls=%fused_computation.15.clone.1 | convolution fusion | flops 405012480 | bytes 16844800 | tf_op jit(solution)/shard_map/while/body/eval_jaxpr/rnskg,nskgd->rskgd/dot_general | solution.py:56
  402.1 1.9 copy-done.3
  404.0 7.7 %constant_dynamic-slice_fusion.5 = f32[1,32,8,4,16,16]{4,5,2,3,1,0:T(8,128)} fusion(f32[4,32,8,4,16,16]{4,5,2,3,1,0:T(8,128)} %get-tuple-element.226, s32[]{:T(128)S(6)} %copy.143), kind=kLoop, calls=%fused_computation.34.clone.1 | loop fusion | bytes 2097156 | tf_op jit(solution)/shard_map/while/body/jit(dynamic_index_in_dim)/dynamic_slice | solution.py:63
  411.7 9.0 %copy.137 = f32[1,32,8,4,16,16]{5,4,2,3,1,0:T(8,128)} copy(f32[1,32,8,4,16,16]{4,5,2,3,1,0:T(8,128)} %constant_dynamic-slice_fusion.5) | data formatting | bytes 2097152 | tf_op jit(solution)/shard_map/while/body/jit(dynamic_index_in_dim)/dynamic_slice | solution.py:63
  421.3 1.2 fusion.58
  422.5 6.9 %fusion.59 = f32[32,8,4,16]{3,1,2,0:T(8,128)S(1)} fusion(f32[1,32,8,4,16,16]{5,4,2,3,1,0:T(8,128)} %copy.137, f32[32,8,4,16]{3,1,2,0:T(8,128)S(1)} %get-tuple-element.197), kind=kLoop, calls=%fused_computation.10.clone.1 | loop fusion | flops 507904 | bytes 1179648 | tf_op jit(solution)/shard_map/while/body/eval_jaxpr/reduce_sum | solution.py:55
  430.1 1.2 fusion.61
  431.3 1.3 constant_dynamic-slice_fusion.6
  432.6 5.7 fusion.62
  438.4 10.8 %bitcast_add_fusion.2 = f32[16,8,4,16,128]{4,0,3,2,1:T(8,128)S(1)} fusion(f32[16,8,4,16,128]{4,0,3,2,1:T(8,128)S(1)} %copy-done.2, f32[32,8,4,16,128]{4,3,1,2,0:T(8,128)S(1)} %fusion.62, f32[32,8,4,16]{0,3,2,1:T(8,128)S(1)} %copy.139, f32[16,32]{1,0:T(8,128)S(1)} %fusion.60, pred[]{:T(512)S(6)} %compare.44), kind=kOutput, calls=%fused_computation.15.clone.1 | convolution fusion | flops 405012480 | bytes 16844800 | tf_op jit(solution)/shard_map/while/body/eval_jaxpr/rnskg,nskgd->rskgd/dot_general | solution.py:56
  449.2 1.9 copy-done.3
  451.1 7.7 %constant_dynamic-slice_fusion.5 = f32[1,32,8,4,16,16]{4,5,2,3,1,0:T(8,128)} fusion(f32[4,32,8,4,16,16]{4,5,2,3,1,0:T(8,128)} %get-tuple-element.226, s32[]{:T(128)S(6)} %copy.143), kind=kLoop, calls=%fused_computation.34.clone.1 | loop fusion | bytes 2097156 | tf_op jit(solution)/shard_map/while/body/jit(dynamic_index_in_dim)/dynamic_slice | solution.py:63
  458.8 9.0 %copy.137 = f32[1,32,8,4,16,16]{5,4,2,3,1,0:T(8,128)} copy(f32[1,32,8,4,16,16]{4,5,2,3,1,0:T(8,128)} %constant_dynamic-slice_fusion.5) | data formatting | bytes 2097152 | tf_op jit(solution)/shard_map/while/body/jit(dynamic_index_in_dim)/dynamic_slice | solution.py:63
  468.4 1.2 fusion.58
  469.6 6.9 %fusion.59 = f32[32,8,4,16]{3,1,2,0:T(8,128)S(1)} fusion(f32[1,32,8,4,16,16]{5,4,2,3,1,0:T(8,128)} %copy.137, f32[32,8,4,16]{3,1,2,0:T(8,128)S(1)} %get-tuple-element.197), kind=kLoop, calls=%fused_computation.10.clone.1 | loop fusion | flops 507904 | bytes 1179648 | tf_op jit(solution)/shard_map/while/body/eval_jaxpr/reduce_sum | solution.py:55
  477.1 1.2 fusion.61
  478.4 1.3 constant_dynamic-slice_fusion.6
  479.7 5.7 fusion.62
  485.4 10.8 %bitcast_add_fusion.2 = f32[16,8,4,16,128]{4,0,3,2,1:T(8,128)S(1)} fusion(f32[16,8,4,16,128]{4,0,3,2,1:T(8,128)S(1)} %copy-done.2, f32[32,8,4,16,128]{4,3,1,2,0:T(8,128)S(1)} %fusion.62, f32[32,8,4,16]{0,3,2,1:T(8,128)S(1)} %copy.139, f32[16,32]{1,0:T(8,128)S(1)} %fusion.60, pred[]{:T(512)S(6)} %compare.44), kind=kOutput, calls=%fused_computation.15.clone.1 | convolution fusion | flops 405012480 | bytes 16844800 | tf_op jit(solution)/shard_map/while/body/eval_jaxpr/rnskg,nskgd->rskgd/dot_general | solution.py:56
  496.2 1.9 copy-done.3
  498.1 7.7 %constant_dynamic-slice_fusion.5 = f32[1,32,8,4,16,16]{4,5,2,3,1,0:T(8,128)} fusion(f32[4,32,8,4,16,16]{4,5,2,3,1,0:T(8,128)} %get-tuple-element.226, s32[]{:T(128)S(6)} %copy.143), kind=kLoop, calls=%fused_computation.34.clone.1 | loop fusion | bytes 2097156 | tf_op jit(solution)/shard_map/while/body/jit(dynamic_index_in_dim)/dynamic_slice | solution.py:63
  505.8 9.0 %copy.137 = f32[1,32,8,4,16,16]{5,4,2,3,1,0:T(8,128)} copy(f32[1,32,8,4,16,16]{4,5,2,3,1,0:T(8,128)} %constant_dynamic-slice_fusion.5) | data formatting | bytes 2097152 | tf_op jit(solution)/shard_map/while/body/jit(dynamic_index_in_dim)/dynamic_slice | solution.py:63
  515.5 1.2 fusion.58
  516.7 6.9 %fusion.59 = f32[32,8,4,16]{3,1,2,0:T(8,128)S(1)} fusion(f32[1,32,8,4,16,16]{5,4,2,3,1,0:T(8,128)} %copy.137, f32[32,8,4,16]{3,1,2,0:T(8,128)S(1)} %get-tuple-element.197), kind=kLoop, calls=%fused_computation.10.clone.1 | loop fusion | flops 507904 | bytes 1179648 | tf_op jit(solution)/shard_map/while/body/eval_jaxpr/reduce_sum | solution.py:55
  524.2 1.2 fusion.61
  525.5 1.3 constant_dynamic-slice_fusion.6
  526.8 5.7 fusion.62
  532.5 10.8 %bitcast_add_fusion.2 = f32[16,8,4,16,128]{4,0,3,2,1:T(8,128)S(1)} fusion(f32[16,8,4,16,128]{4,0,3,2,1:T(8,128)S(1)} %copy-done.2, f32[32,8,4,16,128]{4,3,1,2,0:T(8,128)S(1)} %fusion.62, f32[32,8,4,16]{0,3,2,1:T(8,128)S(1)} %copy.139, f32[16,32]{1,0:T(8,128)S(1)} %fusion.60, pred[]{:T(512)S(6)} %compare.44), kind=kOutput, calls=%fused_computation.15.clone.1 | convolution fusion | flops 405012480 | bytes 16844800 | tf_op jit(solution)/shard_map/while/body/eval_jaxpr/rnskg,nskgd->rskgd/dot_general | solution.py:56
  543.3 1.9 copy-done.3
  545.2 64.7 %psum.15 = f32[16,8,4,16]{0,3,2,1:T(8,128)S(1)} all-reduce(f32[16,8,4,16]{0,3,2,1:T(8,128)S(1)} %get-tuple-element.46), channel_id=1, replica_groups=mesh['groups'=2,'pool'=16] {'pool'}, use_global_device_ids=true, to_apply=%region_19.20 | all-reduce | flops 8192 | bytes 65536 | tf_op jit(solution)/shard_map/psum | solution.py:102
  610.0 61.3 %all-reduce.2.cloned.1.call-done = f32[16,8,4,16,128]{4,0,3,2,1:T(8,128)} async-done(((f32[16,8,4,16,128]{4,0,3,2,1:T(8,128)}), f32[16,8,4,16,128]{4,0,3,2,1:T(8,128)}) %all-reduce.2.cloned.1.call-update) | async-done | bytes 4194320 | tf_op jit(solution)/shard_map/psum | solution.py:102
  671.2 2.9 broadcast_divide_fusion
  674.1 1.4 copy.105
  (99 shorter events, 11.6 us)
Async XLA Ops:
  7.2 58.3 %copy-start = (bf16[16,8,8192]{2,1,0:T(8,128)(2,1)S(1)}, bf16[16,8,8192]{2,1,0:T(8,128)(2,1)}, u32[]{:S(2)}) copy-start(bf16[16,8,8192]{2,1,0:T(8,128)(2,1)} %param.11) | copy-start | bytes 6291460
  40.5 6.8 copy-start.6
  40.5 24.3 %copy-start.7 = (s32[16]{0:T(128)S(1)}, s32[16]{0:T(128)}, u32[]{:S(2)}) copy-start(s32[16]{0:T(128)} %param.12) | copy-start | bytes 196
  40.5 189.0 %all-to-all-start = ((bf16[256,16,1024]{2,1,0:T(8,128)(2,1)}), bf16[256,16,1024]{2,1,0:T(8,128)(2,1)}, u32[]{:S(2)}, u32[]{:S(2)}) async-start(bf16[256,16,1024]{2,1,0:T(8,128)(2,1)} %broadcast_select_fusion), calls=%async_computation | async-start | bytes 16777216 | tf_op jit(solution)/shard_map/all_to_all | solution.py:89
  47.2 624.0 %all-reduce.2.cloned.1.call-start = ((), (), s32[]{:S(2)}) async-start(), calls=%async_computation.1 | async-start | bytes 8388608 | tf_op jit(solution)/shard_map/psum | solution.py:102
  238.4 3.3 copy-start.5
  306.3 2.4 copy-start.4
  385.5 5.7 copy-start.2
  402.1 1.9 copy-start.3
  432.6 5.7 copy-start.2
  449.1 1.9 copy-start.3
  479.7 5.7 copy-start.2
  496.2 1.9 copy-start.3
  526.7 5.7 copy-start.2
  543.3 1.9 copy-start.3
  545.2 130.9 %copy-start.1 = (bf16[16,8,8192]{2,1,0:T(8,128)(2,1)S(1)}, bf16[16,8,8192]{2,1,0:T(8,128)(2,1)}, u32[]{:S(2)}) copy-start(bf16[16,8,8192]{2,1,0:T(8,128)(2,1)} %param.11) | copy-start | bytes 6291460
Sparse Core Ops, SparseCore 0:
  545.4 125.8 all-reduce.1
where the time goes:
time: 689 us; the launch traced here: 683 us
  waiting for transfers between devices  216 us (31%)
  local copies, waits for them, and re-layouts  131 us (19%)
  matrix products  124 us (18%)
  blocking collectives  109 us (16%)
  other arithmetic  81.7 us (12%)
  between operations  14.5 us (2%)
    all_to_all x1, waiting for transfers between devices, local(): lax.all_to_all(outgoing, 'pool', split_axis=0, concat_axis=0, tiled=True)  155 us
    dynamic_slice x12, local copies, waits for them, and re-layouts, accumulate(): lax.scan(block_step, (start_totals, start_numer), (score_blocks, max_bloc...  71.8 us
    psum x1, blocking collectives, local(): summed, numerator = lax.psum((totals, numerator), 'pool')  64.7 us
    psum x1, waiting for transfers between devices, local(): summed, numerator = lax.psum((totals, numerator), 'pool')  61.3 us
    dot_general x1, matrix products, page_scores(): jnp.einsum('nskgd,ntkd->nskgt', picked, key_rows, preferred_element_type=...  58.1 us
    pmax x1, blocking collectives, local(): lax.pmax(local_max.astype(jnp.bfloat16), 'pool').astype(local_max.dtype)  44.2 us
    dot_general x4, matrix products, block_step(): jnp.einsum('rnskg,nskgd->rskgd', spread, page_out, precision=lax.Precisio...  43.2 us
    reduce_sum x8, other arithmetic, block_step(): totals = totals + jnp.sum(spread * jnp.sum(exponent, axis=4)[None], axis=1)  32.2 us
  transfers between devices with their start and end apart: 2, of which 2 were waited for; matrix products, arithmetic and copies ran while one was open for 4% of the time, Pallas kernels for 0%

commit v1 on v0

--- a/solution.py
+++ b/solution.py
@@ -1,6 +1,9 @@
+import functools
 import jax
 import jax.numpy as jnp
 from jax import lax
+from jax.experimental import pallas as pl
+from jax.experimental.pallas import tpu as pltpu
 from jax.sharding import PartitionSpec as P
 
 QH = 64
@@ -9,6 +12,269 @@
 PAGE = 16
 STEPS = 8
 REQS = 16
+KVW = 2 * KVH * HD
+SPAN = 3
+LOW = -1e30
+VMEM_LIMIT = 48 * 1024 * 1024
+F32 = jnp.float32
+BF16 = jnp.bfloat16
+I32 = jnp.int32
+
+
+def decode_kernel(chunk, place, flags, blocks, anchors, deltas, scales, out, rows, staged, sems):
+    step = pl.program_id(0)
+    for head in range(2 * KVH):
+        cols = slice(head * HD, (head + 1) * HD)
+        scale = jnp.broadcast_to(scales[:, head : head + 1], (chunk, HD))
+        anchor = anchors[:, cols].astype(F32)
+        rows[head * PAGE * chunk : head * PAGE * chunk + chunk, :] = anchor
+        for token in range(1, PAGE):
+            start = (head * PAGE + token) * chunk
+            rows[start : start + chunk, :] = anchor + scale * deltas[token - 1, :, cols].astype(F32)
+    for page in range(chunk):
+        picked = [
+            rows[pl.ds(head * PAGE * chunk + page, PAGE, stride=chunk), :]
+            for head in range(2 * KVH)
+        ]
+        staged[place[step * chunk + page]] = jnp.concatenate(picked, axis=1).astype(BF16)
+
+    @pl.when(step == pl.num_programs(0) - 1)
+    def flush():
+        copies = []
+        for owner in range(16):
+            copy = pltpu.make_async_copy(
+                staged.at[pl.ds(blocks[owner] * PAGE, PAGE)],
+                out.at[pl.ds(owner * PAGE, PAGE)],
+                sems.at[owner],
+            )
+            pl.when(flags[owner] > 0)(copy.start)
+            copies.append(copy)
+        for owner in range(16):
+            pl.when(flags[owner] > 0)(copies[owner].wait)
+
+
+def decode_sorted(place, flags, blocks, anchors, deltas, scales):
+    number = anchors.shape[0]
+    chunk = 16
+    return pl.pallas_call(
+        functools.partial(decode_kernel, chunk),
+        grid_spec=pltpu.PrefetchScalarGridSpec(
+            num_scalar_prefetch=3,
+            grid=(number // chunk,),
+            in_specs=[
+                pl.BlockSpec((chunk, KVW), lambda i, *_: (i, 0)),
+                pl.BlockSpec((PAGE - 1, chunk, KVW), lambda i, *_: (0, i, 0)),
+                pl.BlockSpec((chunk, 2 * KVH), lambda i, *_: (i, 0)),
+            ],
+            out_specs=pl.BlockSpec(memory_space=pl.ANY),
+            scratch_shapes=[
+                pltpu.VMEM((2 * KVH * PAGE * chunk, HD), F32),
+                pltpu.VMEM((number, PAGE, KVW), BF16),
+                pltpu.SemaphoreType.DMA((16,)),
+            ],
+        ),
+        out_shape=jax.ShapeDtypeStruct((16 * PAGE, PAGE, KVW), BF16),
+        compiler_params=pltpu.CompilerParams(vmem_limit_bytes=VMEM_LIMIT),
+        name="decode_sorted",
+    )(place, flags, blocks, anchors, deltas, scales)
+
+
+def attend_kernel(base, requests, queries, key_anchor, val_anchor, key_delta, val_delta, scales, out, keys, vals):
+    head = pl.program_id(0)
+    number = key_anchor.shape[0]
+    lane = lax.broadcasted_iota(I32, scales.shape, 1)
+    table = scales[...]
+    key_scale = jnp.sum(jnp.where(lane == head, table, 0.0), axis=1, keepdims=True)
+    val_scale = jnp.sum(jnp.where(lane == head + KVH, table, 0.0), axis=1, keepdims=True)
+    for anchor, delta, scale, kept in (
+        (key_anchor, key_delta, key_scale, keys),
+        (val_anchor, val_delta, val_scale, vals),
+    ):
+        first = anchor[...]
+        kept[0:number, :] = first
+        wide = first.astype(F32)
+        for token in range(1, PAGE):
+            kept[token * number : (token + 1) * number, :] = (
+                wide + scale * delta[token - 1].astype(F32)
+            ).astype(BF16)
+    token_request = jnp.concatenate([requests[...]] * PAGE, axis=1) - base[0]
+    rows = STEPS * QH // KVH
+    eye = lax.broadcasted_iota(I32, (rows, rows), 0) == lax.broadcasted_iota(I32, (rows, rows), 1)
+    pieces = []
+    for slot in range(SPAN):
+        scores = lax.dot_general(
+            queries[slot], keys[...], (((1,), (1,)), ((), ())), preferred_element_type=F32
+        ) * HD ** (-0.5)
+        inside = token_request == slot
+        scores = jnp.where(inside, scores, LOW)
+        top = jnp.max(scores, axis=1, keepdims=True)
+        exponent = jnp.where(inside, jnp.exp(scores - top), 0.0)
+        total = jnp.maximum(jnp.sum(exponent, axis=1, keepdims=True), 1e-30)
+        numer = jnp.dot(exponent.astype(BF16), vals[...], preferred_element_type=F32)
+        mean = (numer * (1.0 / total)).astype(BF16)
+        quarter = rows // 4
+        for part in range(4):
+            out[part, slot * quarter : (slot + 1) * quarter, :] = mean[
+                part * quarter : (part + 1) * quarter
+            ]
+        level = top + jnp.log(total)
+        line = jnp.sum(jnp.where(eye, level, 0.0), axis=0, keepdims=True)
+        for _ in range(3):
+            piece = line.astype(BF16).astype(F32)
+            pieces.append(piece)
+            line = line - piece
+    pieces.append(jnp.zeros((16 - len(pieces), rows), F32))
+    stats = jnp.concatenate(pieces, axis=0).astype(BF16)
+    for part in range(4):
+        out[part, 96:112, :] = stats
+
+
+def attend(base, requests, queries, anchors, deltas, scales):
+    number = anchors.shape[0]
+    rows = STEPS * QH // KVH
+    return pl.pallas_call(
+        attend_kernel,
+        grid_spec=pltpu.PrefetchScalarGridSpec(
+            num_scalar_prefetch=1,
+            grid=(KVH,),
+            in_specs=[
+                pl.BlockSpec((1, number), lambda h, *_: (0, 0)),
+                pl.BlockSpec((SPAN, rows, HD), lambda h, *_: (0, h, 0)),
+                pl.BlockSpec((number, HD), lambda h, *_: (0, h)),
+                pl.BlockSpec((number, HD), lambda h, *_: (0, h + KVH)),
+                pl.BlockSpec((PAGE - 1, number, HD), lambda h, *_: (0, 0, h)),
+                pl.BlockSpec((PAGE - 1, number, HD), lambda h, *_: (0, 0, h + KVH)),
+                pl.BlockSpec((number, 2 * KVH), lambda h, *_: (0, 0)),
+            ],
+            out_specs=pl.BlockSpec((4, 112, HD), lambda h, *_: (h, 0, 0)),
+            scratch_shapes=[
+                pltpu.VMEM((PAGE * number, HD), BF16),
+                pltpu.VMEM((PAGE * number, HD), BF16),
+            ],
+        ),
+        out_shape=jax.ShapeDtypeStruct((16, 112, HD), BF16),
+        compiler_params=pltpu.CompilerParams(vmem_limit_bytes=VMEM_LIMIT),
+        cost_estimate=pl.CostEstimate(
+            flops=SPAN * KVH * rows * number * PAGE * HD * 4,
+            bytes_accessed=5 * 2**20,
+            transcendentals=SPAN * KVH * rows * number * PAGE,
+        ),
+        name="attend",
+    )(base, requests, queries, anchors, anchors, deltas, deltas, scales)
+
+
+def merge_kernel(bases, part, parts, out, level, top, total, numer):
+    quarter = 32
+    row = lax.broadcasted_iota(I32, (quarter, HD), 0)
+    lane = lax.broadcasted_iota(I32, (quarter, HD), 1)
+    mine = lane == row + quarter * part[0]
+    top[...] = jnp.full(top.shape, LOW, F32)
+    total[...] = jnp.zeros(total.shape, F32)
+    numer[...] = jnp.zeros(numer.shape, F32)
+    for sender in range(16):
+        stats = parts[sender, 96:112, :].astype(F32)
+        for slot in range(SPAN):
+            line = stats[3 * slot : 3 * slot + 1] + (
+                stats[3 * slot + 1 : 3 * slot + 2] + stats[3 * slot + 2 : 3 * slot + 3]
+            )
+            column = jnp.sum(jnp.where(mine, line, 0.0), axis=1, keepdims=True)
+            column = jnp.broadcast_to(column, (quarter, HD))
+            level[sender * SPAN + slot] = column
+            request = bases[sender] + slot
+            top[request] = jnp.maximum(top[request], column)
+    for sender in range(16):
+        for slot in range(SPAN):
+            request = bases[sender] + slot
+            weight = jnp.exp(level[sender * SPAN + slot] - top[request])
+            mean = parts[sender, slot * quarter : (slot + 1) * quarter, :].astype(F32)
+            total[request] += weight
+            numer[request] += weight * mean
+    for request in range(REQS):
+        result = (numer[request] / total[request]).astype(BF16)
+        for group in range(4):
+            out[request, :, group * HD : (group + 1) * HD] = result[
+                group * STEPS : (group + 1) * STEPS
+            ]
+
+
+def merge(bases, part, parts):
+    return pl.pallas_call(
+        merge_kernel,
+        grid_spec=pltpu.PrefetchScalarGridSpec(
+            num_scalar_prefetch=2,
+            grid=(1,),
+            in_specs=[pl.BlockSpec((16, 112, HD), lambda i, *_: (0, 0, 0))],
+            out_specs=pl.BlockSpec((REQS, STEPS, 4 * HD), lambda i, *_: (0, 0, 0)),
+            scratch_shapes=[
+                pltpu.VMEM((16 * SPAN, 32, HD), F32),
+                pltpu.VMEM((REQS, 32, HD), F32),
+                pltpu.VMEM((REQS, 32, HD), F32),
+                pltpu.VMEM((REQS, 32, HD), F32),
+            ],
+        ),
+        out_shape=jax.ShapeDtypeStruct((REQS, STEPS, 4 * HD), BF16),
+        compiler_params=pltpu.CompilerParams(vmem_limit_bytes=VMEM_LIMIT),
+        name="merge",
+    )(bases, part, parts)
+
+
+def assemble_kernel(flags, blocks, arrived, out, sems):
+    copies = []
+    for sender in range(16):
+        copy = pltpu.make_async_copy(
+            arrived.at[pl.ds(sender * PAGE, PAGE)],
+            out.at[pl.ds(blocks[sender] * PAGE, PAGE)],
+            sems.at[sender],
+        )
+        pl.when(flags[sender] > 0)(copy.start)
+        copies.append(copy)
+    for sender in range(16):
+        pl.when(flags[sender] > 0)(copies[sender].wait)
+
+
+def assemble(flags, blocks, arrived, number):
+    return pl.pallas_call(
+        assemble_kernel,
+        grid_spec=pltpu.PrefetchScalarGridSpec(
+            num_scalar_prefetch=2,
+            grid=(1,),
+            in_specs=[pl.BlockSpec(memory_space=pl.ANY)],
+            out_specs=pl.BlockSpec(memory_space=pl.ANY),
+            scratch_shapes=[pltpu.SemaphoreType.DMA((16,))],
+        ),
+        out_shape=jax.ShapeDtypeStruct((number, PAGE, KVW), BF16),
+        name="assemble",
+    )(flags, blocks, arrived)
+
+
+def local_slab(anchors, deltas, scales, queries, lengths, page_owner):
+    position = lax.axis_index("pool")
+    number = anchors.shape[0]
+    by_token = jnp.transpose(deltas, (1, 0, 2))
+    ends = jnp.cumsum(lengths)
+    owners = lax.dynamic_slice_in_dim(page_owner, position * number, number, 0)
+    order = jnp.arange(number, dtype=I32)
+    ahead = (owners[None, :] < owners[:, None]) | (
+        (owners[None, :] == owners[:, None]) & (order[None, :] < order[:, None])
+    )
+    place = jnp.sum(ahead.astype(I32), axis=1)
+    devices = jnp.arange(16, dtype=I32)
+    sent = jnp.any(owners[None, :] == devices[:, None], axis=1).astype(I32)
+    slabs = decode_sorted(place, sent, jnp.cumsum(sent) - sent, anchors, by_token, scales)
+    arrived = lax.all_to_all(slabs, "pool", split_axis=0, concat_axis=0, tiled=True)
+    taken = jnp.any((page_owner == position).reshape(16, number), axis=1).astype(I32)
+    bases = jnp.sum((devices[:, None] * number >= ends[None, :]).astype(I32), axis=1)
+    bases = jnp.minimum(bases, REQS - SPAN)
+    base = lax.dynamic_slice_in_dim(bases, position, 1, 0)
+    pages = position * number + order
+    requests = jnp.sum((pages[:, None] >= ends[None, :]).astype(I32), axis=1)[None, :]
+    near = lax.dynamic_slice_in_dim(queries, base[0], SPAN, 0)
+    near = near.reshape(SPAN, STEPS, QH, HD).transpose(0, 2, 1, 3).reshape(SPAN, QH * STEPS, HD)
+    parts = attend(base, requests, near, anchors, by_token, scales)
+    swapped = lax.all_to_all(parts, "pool", split_axis=0, concat_axis=0, tiled=True)
+    attention = merge(bases, (position % 4)[None].astype(I32), swapped)
+    cache = assemble(taken, jnp.cumsum(taken) - taken, arrived, number)
+    return (cache, attention)
 
 
 def decode_pages(anchors, deltas, scales):
@@ -114,8 +380,9 @@
         P("groups"),
         P("groups"),
     )
+    slab = mesh.shape["pool"] == 16
     return jax.shard_map(
-        local,
+        local_slab if slab else local,
         mesh=mesh,
         in_specs=placed,
         out_specs=(P(("groups", "pool"), None, None), P("groups", None, "pool")),

time: 689 us -> 355 us (0.52)
  Pallas kernels: 0 us -> 149 us
  matrix products: 124 us -> 0 us
  local copies, waits for them, and re-layouts: 131 us -> 7.72 us
  blocking collectives: 109 us -> 0 us
  other arithmetic: 81.7 us -> 2.27 us
  waiting for transfers between devices: 216 us -> 181 us
  between operations: 14.5 us -> 2.69 us
    pallas_call x0 -> x4, Pallas kernels: none -> 149 us  [the longest x1 129 us: assemble(): pl.pallas_call(assemble_kernel, grid_spec=pltpu.PrefetchScalarGridSpec(nu...]
    dot_general x9 -> x0, matrix products: 124 us -> none  [the longest x1 58.1 us: page_scores(): jnp.einsum('nskgd,ntkd->nskgt', picked, key_rows, preferred_element_type=...]
    dynamic_slice x13 -> x2, local copies, waits for them, and re-layouts: 72.6 us -> 0.67 us  [the longest x1 0.59 us: local_slab(): base = lax.dynamic_slice_in_dim(bases, position, 1, 0)]
    psum x1 -> x0, blocking collectives: 64.7 us -> none  [local(): summed, numerator = lax.psum((totals, numerator), 'pool')]
    psum x1 -> x0, waiting for transfers between devices: 61.3 us -> none  [local(): summed, numerator = lax.psum((totals, numerator), 'pool')]
    pmax x1 -> x0, blocking collectives: 44.2 us -> none  [local(): lax.pmax(local_max.astype(jnp.bfloat16), 'pool').astype(local_max.dtype)]
    reduce_sum x13 -> x3, other arithmetic: 33.3 us -> 0.45 us  [the longest x1 0.18 us: local_slab(): jnp.sum((devices[:, None] * number >= ends[None, :]).astype(I32), axis=1)]
    gather x7 -> x0, local copies, waits for them, and re-layouts: 27.7 us -> none  [the longest x1 10.8 us: local(): outgoing = jnp.take(pages, sources, axis=0)]
  transfers between devices with their start and end apart: 2 -> 2, of which waited for: 2 -> 2; matrix products, arithmetic and copies ran while one was open for 4% -> 1% of each run, Pallas kernels for 0% -> 2%
where the time goes in v1:
time: 355 us
  waiting for transfers between devices  181 us (51%)
  Pallas kernels  149 us (42%)
  starting transfers between devices  12.2 us (3%)
  local copies, waits for them, and re-layouts  7.72 us (2%)
    all_to_all x1, waiting for transfers between devices, local_slab(): lax.all_to_all(slabs, 'pool', split_axis=0, concat_axis=0, tiled=True)  179 us
    pallas_call x1, Pallas kernels, assemble(): pl.pallas_call(assemble_kernel, grid_spec=pltpu.PrefetchScalarGridSpec(nu...  129 us
    pallas_call x1, Pallas kernels, attend(): pl.pallas_call(attend_kernel, grid_spec=pltpu.PrefetchScalarGridSpec(num_...  10.8 us
  transfers between devices with their start and end apart: 2, of which 2 were waited for; matrix products, arithmetic and copies ran while one was open for 1% of the time, Pallas kernels for 2%

profile of v1, /device:TPU:11, one launch (start us, length us, event | category | flops | bytes accessed | tf_op | source)
XLA Modules:
  0.0 354.9 jit_solution(17625141780909386534)
XLA Ops:
  0.6 0.0 copy-start
  0.7 0.9 copy.21
  1.6 0.1 reduce.2
  1.7 0.2 convert_reduce_fusion.2
  1.9 0.6 dynamic_slice.10.base
  3.8 0.8 copy.20.scales
  4.6 0.1 convert_reduce_fusion.1
  5.3 0.0 copy-done
  5.4 0.0 copy-start.1
  5.4 2.1 copy-done.1
  7.5 0.0 copy-start.3
  7.5 0.9 copy-done.3
  8.4 0.0 copy-start.5
  8.4 0.0 copy-start.4
  8.4 10.8 %attend.1 = bf16[16,112,128]{2,1,0:T(8,128)(2,1)} custom-call(s32[1]{0:T(128)} %dynamic_slice.10.base, s32[1,128]{1,0:T(1,128)S(1)} %bitcast.20, bf16[3,512,128]{2,1,0:T(8,128)(2,1)S(1)} %dynamic-slice_bitcast_fusion.queries, bf16[128,1024]{1,0:T(8,128)(2,1)S(1)} %copy-done.3, bf16[128,1024]{1,0:T(8,128)(2,1)S(1)} %copy-done.3, ...), custom_call_target="tpu_custom_call" | custom-call | flops 1610612736 | bytes 5242880 | tf_op jit(solution)/shard_map/attend/pallas_call | solution.py:135
  19.2 6.6 %all-to-all-start.1 = ((bf16[16,112,128]{2,1,0:T(8,128)(2,1)}), bf16[16,112,128]{2,1,0:T(8,128)(2,1)S(1)}, u32[]{:S(2)}, u32[]{:S(2)}) async-start(bf16[16,112,128]{2,1,0:T(8,128)(2,1)} %attend.1), calls=%async_computation.1 | async-start | bytes 917504 | tf_op jit(solution)/shard_map/all_to_all | solution.py:274
  25.8 0.0 copy-done.5
  25.8 0.1 dynamic_slice.9
  25.8 0.1 fusion.2
  26.0 0.1 copy.19
  26.1 0.1 reduce.1
  26.2 0.2 convert_reduce_fusion.place
  26.4 0.0 copy-done.4
  26.4 0.0 copy-start.2
  26.4 2.1 copy-done.2
  28.5 7.0 %decode_sorted.1 = bf16[256,16,1024]{2,1,0:T(8,128)(2,1)} custom-call(s32[128]{0:T(128)S(1)} %convert_reduce_fusion.place, s32[16]{0:T(128)S(1)} %get-tuple-element.3.flags, s32[16]{0:T(128)S(1)} %convert_subtract_fusion.blocks, bf16[128,1024]{1,0:T(8,128)(2,1)S(1)} %copy-done.4, bf16[15,128,1024]{2,1,0:T(8,128)(2,1)S(1)} %bitcast.19, f32[128,8]{1,0:T(8,128)S(1)} %copy.20.scales), custom_call_target="tpu_custom_call" | custom-call | tf_op jit(solution)/shard_map/decode_sorted/pallas_call | solution.py:59
  35.5 2.4 all-to-all-done.1.parts
  37.9 5.7 %all-to-all-start = ((bf16[256,16,1024]{2,1,0:T(8,128)(2,1)}), bf16[256,16,1024]{2,1,0:T(8,128)(2,1)}, u32[]{:S(2)}, u32[]{:S(2)}) async-start(bf16[256,16,1024]{2,1,0:T(8,128)(2,1)} %decode_sorted.1), calls=%async_computation | async-start | bytes 16777216 | tf_op jit(solution)/shard_map/all_to_all | solution.py:264
  43.6 0.1 bitcast_reduce_fusion
  43.7 0.5 convert_bitcast_fusion.1
  44.2 0.1 copy.18
  44.4 0.1 reduce
  44.5 0.6 convert_subtract_fusion.1.blocks
  45.1 1.8 merge.1
  46.9 179.1 %all-to-all-done.arrived = bf16[256,16,1024]{2,1,0:T(8,128)(2,1)} async-done(((bf16[256,16,1024]{2,1,0:T(8,128)(2,1)}), bf16[256,16,1024]{2,1,0:T(8,128)(2,1)}, u32[]{:S(2)}, u32[]{:S(2)}) %all-to-all-start) | async-done | bytes 8388640 | tf_op jit(solution)/shard_map/all_to_all | solution.py:264
  226.0 129.0 %assemble.1 = bf16[128,16,1024]{2,1,0:T(8,128)(2,1)} custom-call(s32[16]{0:T(128)} %get-tuple-element.5.flags, s32[16]{0:T(128)} %convert_subtract_fusion.1.blocks, bf16[256,16,1024]{2,1,0:T(8,128)(2,1)} %all-to-all-done.arrived), custom_call_target="tpu_custom_call" | custom-call | tf_op jit(solution)/shard_map/assemble/pallas_call | solution.py:236
  (9 shorter events, 0.2 us)
Async XLA Ops:
  0.6 4.7 %copy-start = (bf16[16,8,8192]{2,1,0:T(8,128)(2,1)S(1)}, bf16[16,8,8192]{2,1,0:T(8,128)(2,1)}, u32[]{:S(2)}) copy-start(bf16[16,8,8192]{2,1,0:T(8,128)(2,1)} %param.9) | copy-start | bytes 6291460
  5.4 2.1 copy-start.1
  7.5 0.9 copy-start.3
  8.4 17.3 %copy-start.5 = (s32[2048]{0:T(1024)S(1)}, s32[2048]{0:T(1024)}, u32[]{:S(2)}) copy-start(s32[2048]{0:T(1024)} %param.11) | copy-start | bytes 24580
  8.4 18.0 %copy-start.4 = (bf16[128,1024]{1,0:T(8,128)(2,1)S(1)}, bf16[128,1024]{1,0:T(8,128)(2,1)}, u32[]{:S(2)}) copy-start(bf16[128,1024]{1,0:T(8,128)(2,1)} %val_anchor.1) | copy-start | bytes 786436
  19.2 18.7 %all-to-all-start.1 = ((bf16[16,112,128]{2,1,0:T(8,128)(2,1)}), bf16[16,112,128]{2,1,0:T(8,128)(2,1)S(1)}, u32[]{:S(2)}, u32[]{:S(2)}) async-start(bf16[16,112,128]{2,1,0:T(8,128)(2,1)} %attend.1), calls=%async_computation.1 | async-start | bytes 917504 | tf_op jit(solution)/shard_map/all_to_all | solution.py:274
  26.4 2.1 copy-start.2
  37.9 188.0 %all-to-all-start = ((bf16[256,16,1024]{2,1,0:T(8,128)(2,1)}), bf16[256,16,1024]{2,1,0:T(8,128)(2,1)}, u32[]{:S(2)}, u32[]{:S(2)}) async-start(bf16[256,16,1024]{2,1,0:T(8,128)(2,1)} %decode_sorted.1), calls=%async_computation | async-start | bytes 16777216 | tf_op jit(solution)/shard_map/all_to_all | solution.py:264

commit v2 on v1

--- a/solution.py
+++ b/solution.py
@@ -218,18 +218,24 @@
     )(bases, part, parts)
 
 
-def assemble_kernel(flags, blocks, arrived, out, sems):
-    copies = []
-    for sender in range(16):
-        copy = pltpu.make_async_copy(
-            arrived.at[pl.ds(sender * PAGE, PAGE)],
-            out.at[pl.ds(blocks[sender] * PAGE, PAGE)],
-            sems.at[sender],
-        )
-        pl.when(flags[sender] > 0)(copy.start)
-        copies.append(copy)
-    for sender in range(16):
-        pl.when(flags[sender] > 0)(copies[sender].wait)
+def assemble_kernel(flags, blocks, arrived, out, staged, in_sems, out_sems):
+    reads, writes = [], []
+    for sender in range(16):
+        rows = pl.ds(blocks[sender] * PAGE, PAGE)
+        source = arrived.at[pl.ds(sender * PAGE, PAGE)]
+        reads.append(pltpu.make_async_copy(source, staged.at[rows], in_sems.at[sender]))
+        writes.append(pltpu.make_async_copy(staged.at[rows], out.at[rows], out_sems.at[sender]))
+    for sender in range(16):
+        pl.when(flags[sender] > 0)(reads[sender].start)
+    for sender in range(16):
+
+        @pl.when(flags[sender] > 0)
+        def forward():
+            reads[sender].wait()
+            writes[sender].start()
+
+    for sender in range(16):
+        pl.when(flags[sender] > 0)(writes[sender].wait)
 
 
 def assemble(flags, blocks, arrived, number):
@@ -240,9 +246,14 @@
             grid=(1,),
             in_specs=[pl.BlockSpec(memory_space=pl.ANY)],
             out_specs=pl.BlockSpec(memory_space=pl.ANY),
-            scratch_shapes=[pltpu.SemaphoreType.DMA((16,))],
+            scratch_shapes=[
+                pltpu.VMEM((number, PAGE, KVW), BF16),
+                pltpu.SemaphoreType.DMA((16,)),
+                pltpu.SemaphoreType.DMA((16,)),
+            ],
         ),
         out_shape=jax.ShapeDtypeStruct((number, PAGE, KVW), BF16),
+        compiler_params=pltpu.CompilerParams(vmem_limit_bytes=VMEM_LIMIT),
         name="assemble",
     )(flags, blocks, arrived)
 

time: 355 us -> 231 us (0.65)
  Pallas kernels: 149 us -> 23.8 us
    pallas_call x1, Pallas kernels: 129 us -> 4.27 us  [assemble(): pl.pallas_call(assemble_kernel, grid_spec=pltpu.PrefetchScalarGridSpec(nu...]
  transfers between devices with their start and end apart: 2 -> 2, of which waited for: 2 -> 2; matrix products, arithmetic and copies ran while one was open for 1% -> 0% of each run, Pallas kernels for 2% -> 4%
where the time goes in v2:
time: 231 us; the launch traced here: 230 us
  waiting for transfers between devices  183 us (79%)
  Pallas kernels  23.8 us (10%)
  starting transfers between devices  12.2 us (5%)
  local copies, waits for them, and re-layouts  7.73 us (3%)
  between operations  2.7 us (1%)
    all_to_all x1, waiting for transfers between devices, local_slab(): lax.all_to_all(slabs, 'pool', split_axis=0, concat_axis=0, tiled=True)  180 us
    pallas_call x1, Pallas kernels, attend(): pl.pallas_call(attend_kernel, grid_spec=pltpu.PrefetchScalarGridSpec(num_...  10.8 us
    pallas_call x1, Pallas kernels, decode_sorted(): pl.pallas_call(functools.partial(decode_kernel, chunk), grid_spec=pltpu.P...  6.99 us
    all_to_all x1, starting transfers between devices, local_slab(): lax.all_to_all(parts, 'pool', split_axis=0, concat_axis=0, tiled=True)  6.56 us
    unnamed x13, local copies, waits for them, and re-layouts  5.97 us
    all_to_all x1, starting transfers between devices, local_slab(): lax.all_to_all(slabs, 'pool', split_axis=0, concat_axis=0, tiled=True)  5.68 us
  transfers between devices with their start and end apart: 2, of which 2 were waited for; matrix products, arithmetic and copies ran while one was open for 0% of the time, Pallas kernels for 4%

profile of v2, /device:TPU:11, one launch (start us, length us, event | category | flops | bytes accessed | tf_op | source)
XLA Modules:
  0.0 230.2 jit_solution(13506701672735148261)
XLA Ops:
  0.6 0.0 copy-start
  0.7 0.9 copy.21
  1.6 0.1 reduce.2
  1.7 0.2 convert_reduce_fusion.2
  1.9 0.6 dynamic_slice.10.base
  3.8 0.8 copy.20.scales
  4.6 0.1 convert_reduce_fusion.1
  5.3 0.0 copy-done
  5.4 0.0 copy-start.1
  5.4 2.1 copy-done.1
  7.5 0.0 copy-start.3
  7.5 0.9 copy-done.3
  8.4 0.0 copy-start.5
  8.4 0.0 copy-start.4
  8.4 10.8 %attend.1 = bf16[16,112,128]{2,1,0:T(8,128)(2,1)} custom-call(s32[1]{0:T(128)} %dynamic_slice.10.base, s32[1,128]{1,0:T(1,128)S(1)} %bitcast.20, bf16[3,512,128]{2,1,0:T(8,128)(2,1)S(1)} %dynamic-slice_bitcast_fusion.queries, bf16[128,1024]{1,0:T(8,128)(2,1)S(1)} %copy-done.3, bf16[128,1024]{1,0:T(8,128)(2,1)S(1)} %copy-done.3, ...), custom_call_target="tpu_custom_call" | custom-call | flops 1610612736 | bytes 5242880 | tf_op jit(solution)/shard_map/attend/pallas_call | solution.py:135
  19.2 6.6 %all-to-all-start.1 = ((bf16[16,112,128]{2,1,0:T(8,128)(2,1)}), bf16[16,112,128]{2,1,0:T(8,128)(2,1)S(1)}, u32[]{:S(2)}, u32[]{:S(2)}) async-start(bf16[16,112,128]{2,1,0:T(8,128)(2,1)} %attend.1), calls=%async_computation.1 | async-start | bytes 917504 | tf_op jit(solution)/shard_map/all_to_all | solution.py:285
  25.8 0.0 copy-done.5
  25.8 0.1 dynamic_slice.9
  25.8 0.1 fusion.2
  26.0 0.1 copy.19
  26.1 0.1 reduce.1
  26.2 0.2 convert_reduce_fusion.place
  26.4 0.0 copy-done.4
  26.4 0.0 copy-start.2
  26.4 2.1 copy-done.2
  28.5 7.0 %decode_sorted.1 = bf16[256,16,1024]{2,1,0:T(8,128)(2,1)} custom-call(s32[128]{0:T(128)S(1)} %convert_reduce_fusion.place, s32[16]{0:T(128)S(1)} %get-tuple-element.3.flags, s32[16]{0:T(128)S(1)} %convert_subtract_fusion.blocks, bf16[128,1024]{1,0:T(8,128)(2,1)S(1)} %copy-done.4, bf16[15,128,1024]{2,1,0:T(8,128)(2,1)S(1)} %bitcast.19, f32[128,8]{1,0:T(8,128)S(1)} %copy.20.scales), custom_call_target="tpu_custom_call" | custom-call | tf_op jit(solution)/shard_map/decode_sorted/pallas_call | solution.py:59
  35.5 2.4 %all-to-all-done.1.parts = bf16[16,112,128]{2,1,0:T(8,128)(2,1)S(1)} async-done(((bf16[16,112,128]{2,1,0:T(8,128)(2,1)}), bf16[16,112,128]{2,1,0:T(8,128)(2,1)S(1)}, u32[]{:S(2)}, u32[]{:S(2)}) %all-to-all-start.1) | async-done | bytes 458784 | tf_op jit(solution)/shard_map/all_to_all | solution.py:285
  37.9 5.7 %all-to-all-start = ((bf16[256,16,1024]{2,1,0:T(8,128)(2,1)}), bf16[256,16,1024]{2,1,0:T(8,128)(2,1)}, u32[]{:S(2)}, u32[]{:S(2)}) async-start(bf16[256,16,1024]{2,1,0:T(8,128)(2,1)} %decode_sorted.1), calls=%async_computation | async-start | bytes 16777216 | tf_op jit(solution)/shard_map/all_to_all | solution.py:275
  43.6 0.1 bitcast_reduce_fusion
  43.7 0.1 copy.18
  43.8 0.1 reduce
  44.0 1.8 merge.1
  45.8 180.2 %all-to-all-done.arrived = bf16[256,16,1024]{2,1,0:T(8,128)(2,1)} async-done(((bf16[256,16,1024]{2,1,0:T(8,128)(2,1)}), bf16[256,16,1024]{2,1,0:T(8,128)(2,1)}, u32[]{:S(2)}, u32[]{:S(2)}) %all-to-all-start) | async-done | bytes 8388640 | tf_op jit(solution)/shard_map/all_to_all | solution.py:275
  226.0 4.3 %assemble.1 = bf16[128,16,1024]{2,1,0:T(8,128)(2,1)} custom-call(s32[16]{0:T(128)S(1)} %get-tuple-element.5.flags, s32[16]{0:T(128)S(1)} %convert_subtract_fusion.1.blocks, bf16[256,16,1024]{2,1,0:T(8,128)(2,1)} %all-to-all-done.arrived), custom_call_target="tpu_custom_call" | custom-call | tf_op jit(solution)/shard_map/assemble/pallas_call | solution.py:242
  (11 shorter events, 0.2 us)
Async XLA Ops:
  0.6 4.7 %copy-start = (bf16[16,8,8192]{2,1,0:T(8,128)(2,1)S(1)}, bf16[16,8,8192]{2,1,0:T(8,128)(2,1)}, u32[]{:S(2)}) copy-start(bf16[16,8,8192]{2,1,0:T(8,128)(2,1)} %param.9) | copy-start | bytes 6291460
  5.4 2.1 copy-start.1
  7.5 0.9 copy-start.3
  8.4 17.3 %copy-start.5 = (s32[2048]{0:T(1024)S(1)}, s32[2048]{0:T(1024)}, u32[]{:S(2)}) copy-start(s32[2048]{0:T(1024)} %param.11) | copy-start | bytes 24580
  8.4 18.0 %copy-start.4 = (bf16[128,1024]{1,0:T(8,128)(2,1)S(1)}, bf16[128,1024]{1,0:T(8,128)(2,1)}, u32[]{:S(2)}) copy-start(bf16[128,1024]{1,0:T(8,128)(2,1)} %val_anchor.1) | copy-start | bytes 786436
  19.2 18.7 %all-to-all-start.1 = ((bf16[16,112,128]{2,1,0:T(8,128)(2,1)}), bf16[16,112,128]{2,1,0:T(8,128)(2,1)S(1)}, u32[]{:S(2)}, u32[]{:S(2)}) async-start(bf16[16,112,128]{2,1,0:T(8,128)(2,1)} %attend.1), calls=%async_computation.1 | async-start | bytes 917504 | tf_op jit(solution)/shard_map/all_to_all | solution.py:285
  26.4 2.1 copy-start.2
  37.9 188.0 %all-to-all-start = ((bf16[256,16,1024]{2,1,0:T(8,128)(2,1)}), bf16[256,16,1024]{2,1,0:T(8,128)(2,1)}, u32[]{:S(2)}, u32[]{:S(2)}) async-start(bf16[256,16,1024]{2,1,0:T(8,128)(2,1)} %decode_sorted.1), calls=%async_computation | async-start | bytes 16777216 | tf_op jit(solution)/shard_map/all_to_all | solution.py:275
